TPU v7x, 128 devices: a whole 4x4x4 slice. The times are simulated.
128 devices in a mesh: head: 4 (over x_lo, core), expert: 32 (over z, y, x_hi).
Axes of the slice: x: 4 (x_hi: 2, x_lo: 2; x = x_hi * 2 + x_lo), y: 4, z: 4, core: 2. Of those that a mesh axis runs over, the one named last changes fastest.
Arguments:
- attn: bfloat16 [4096, 4096], P('expert', 'head'), may hold values from -6 to 6
- o_weight: bfloat16 [4096, 4096], P('head'), may hold values from -0.09375 to 0.09375
- residual: bfloat16 [4096, 4096], P('expert'), may hold values from -6 to 6
- expert_ids: int32 [4096, 8], P('expert'), may hold values from 0 to 31, all different within a row; in each aligned block of 128 rows (0 to 127, 128 to 255, ...) at most 64 rows name the same one
- route_weight: bfloat16 [4096, 8], P('expert'), may hold values from 0.099609375 to 1
- gate_weight: bfloat16 [32, 4096, 1536], P('expert', None, 'head'), may hold values from -0.09375 to 0.09375
- up_weight: bfloat16 [32, 4096, 1536], P('expert', None, 'head'), may hold values from -0.09375 to 0.09375
Outputs:
- gram: float32 [32, 1536, 1536], P('expert', 'head')
Inputs may be any that keep to these rules, and one draw needn't show every extreme that they name: `expert_ids`: among the 128 rows of one device no expert is named more than 64 times, a bound that some block reaches; each row names 8 different experts.
All inputs are finite; a program needn't handle non-finite values.
Results may differ from a plain program's by a relative error of at most 0.0065.
Values may be sent and summed in bfloat16 or wider, within the bound.
No kernel may reach another device: no remote copies, remote signals or barrier semaphores. Data moves between devices by JAX's collectives and lax.ppermute only.
A program may use at most 128 MiB of HBM per device.

v0:
```python
import jax
import jax.numpy as jnp
from jax import lax
from jax.sharding import PartitionSpec as P


def body(attn, o_weight, residual, expert_ids, route_weight, gate_weight, up_weight):
    partial_value = jnp.dot(attn, o_weight, preferred_element_type=jnp.float32)
    width = residual.shape[1]
    mixed = residual.astype(jnp.float32) + lax.psum(partial_value, "head")
    squares = jnp.sum(mixed * mixed, axis=1)
    normed = (mixed * lax.rsqrt(squares / width + 1e-06)[:, None]).astype(jnp.bfloat16)
    owners = lax.axis_size("expert")
    tok_rows = expert_ids.shape[0]
    picks = expert_ids.shape[1]
    capacity = min(tok_rows, 2 * tok_rows * picks // owners)
    flat_ids = expert_ids.reshape(-1)
    hits = (flat_ids[:, None] == jnp.arange(owners, dtype=jnp.int32)[None, :]).astype(jnp.int32)
    before = jnp.cumsum(hits, axis=0) - hits
    rank = jnp.sum(before * hits, axis=1)
    slot_of = flat_ids * capacity + rank
    select = jnp.arange(owners * capacity, dtype=jnp.int32)[:, None] == slot_of[None, :]
    pick_rows = jnp.sum(
        select.reshape(owners * capacity, tok_rows, picks).astype(jnp.float32), axis=2
    ).astype(jnp.bfloat16)
    outgoing = jnp.dot(pick_rows, normed, preferred_element_type=jnp.float32).astype(jnp.bfloat16)
    out_weight = jnp.dot(
        select.astype(jnp.bfloat16), route_weight.reshape(-1), preferred_element_type=jnp.float32
    ).astype(jnp.bfloat16)
    outgoing = outgoing.reshape(owners, capacity, outgoing.shape[1])
    out_weight = out_weight.reshape(owners, capacity)
    received, got_weight = (
        lax.all_to_all(outgoing, "expert", split_axis=0, concat_axis=0, tiled=True),
        lax.all_to_all(out_weight, "expert", split_axis=0, concat_axis=0, tiled=True),
    )
    received = received.reshape(owners * capacity, received.shape[2])
    weights = got_weight.reshape(-1).astype(jnp.float32)
    w_gate = gate_weight[0]
    w_up = up_weight[0]
    gate = jnp.dot(received, w_gate, preferred_element_type=jnp.float32)
    up = jnp.dot(received, w_up, preferred_element_type=jnp.float32)
    keys = (jax.nn.silu(gate) * up).astype(jnp.bfloat16)
    scaled = (keys.astype(jnp.float32) * weights[:, None]).astype(jnp.bfloat16)
    total = jnp.sum(weights)
    block = lax.dot_general(
        scaled,
        lax.all_gather(keys, "head", axis=1, tiled=True),
        (((0,), (0,)), ((), ())),
        preferred_element_type=jnp.float32,
    )
    return (block / total)[None]


def solution(mesh):
    return jax.shard_map(
        body,
        mesh=mesh,
        in_specs=(
            P("expert", "head"),
            P("head", None),
            P("expert", None),
            P("expert", None),
            P("expert", None),
            P("expert", None, "head"),
            P("expert", None, "head"),
        ),
        out_specs=P("expert", "head", None),
        check_vma=False,
    )
```

profile of v0, /device:TPU:1, one launch (start us, length us, event | category | flops | bytes accessed | tf_op | source)
XLA Modules:
  0.0 379.8 jit_solution(18009387903659166094)
XLA Ops:
  6.5 6.2 %fusion.16 = f32[128,4096]{1,0:T(8,128)} fusion(bf16[128,1024]{1,0:T(8,128)(2,1)} %param.7, bf16[1024,4096]{1,0:T(8,128)(2,1)} %param.8), kind=kOutput, calls=%fused_computation.33 | convolution fusion | flops 1073741824 | bytes 10747904 | tf_op jit(solution)/shard_map/dot_general | solution.py:8
  12.8 0.1 copy.33
  12.9 0.1 eq.50
  13.0 0.1 eq.46
  13.1 9.0 %reduce-window.6 = s32[32,8,128]{2,1,0:T(8,128)S(1)} reduce-window(s32[32,8,128]{2,1,0:T(8,128)S(1)} %fusion.15, s32[]{:T(128)} %constant.7.clone.1), window={size=1x1x128 pad=0_0x0_0x127_0}, to_apply=%region_0.0 | reduce-window | flops 4161536 | bytes 262148 | tf_op jit(solution)/shard_map/reduce-window
  22.2 0.1 slice.8
  22.3 0.1 copy.35
  22.5 0.1 broadcast_add_fusion
  22.7 0.1 reduce_sum.39
  22.8 11.5 %convert_reduce_fusion = bf16[2048,128]{1,0:T(8,128)(2,1)} fusion(s32[128,8]{0,1:T(8,128)S(1)} %multiply_add_fusion.1), kind=kLoop, calls=%fused_computation.2 | loop fusion | flops 6029312 | bytes 528384 | tf_op jit(solution)/shard_map/reduce_sum | solution.py:23
  34.3 39.5 %all-reduce.2.cloned.1.call-done = f32[128,4096]{1,0:T(8,128)} async-done(((f32[128,4096]{1,0:T(8,128)}), f32[128,4096]{1,0:T(8,128)}) %all-reduce.2.cloned.1.call-update) | async-done | bytes 2097168 | tf_op jit(solution)/shard_map/psum | solution.py:10
  73.8 2.2 multiply_reduce_fusion
  76.0 12.3 %convolution_convert_fusion = bf16[2048,4096]{1,0:T(8,128)(2,1)} fusion(f32[128,4096]{1,0:T(8,128)} %all-reduce.2.cloned.1.call-done, bf16[128,4096]{1,0:T(8,128)(2,1)} %param.9, f32[128]{0:T(128)S(1)} %add_rsqrt_fusion, bf16[2048,128]{1,0:T(8,128)(2,1)} %convert_reduce_fusion), kind=kOutput, calls=%fused_computation | convolution fusion | flops 2157969408 | bytes 20447744 | tf_op jit(solution)/shard_map/dot_general | solution.py:26
  88.4 196.1 %all_to_all.15 = bf16[32,64,4096]{2,1,0:T(8,128)(2,1)S(1)} all-to-all(bf16[32,64,4096]{2,1,0:T(8,128)(2,1)} %bitcast.38), channel_id=1, replica_groups=mesh['head'=4,'expert'=32] {'expert'}, dimensions={0} | all-to-all | bytes 33554432 | tf_op jit(solution)/shard_map/all_to_all | solution.py:33
  284.5 8.9 %fusion.3 = f32[2048,384]{1,0:T(8,128)S(1)} fusion(bf16[2048,4096]{1,0:T(8,128)(2,1)S(1)} %bitcast.39, bf16[1,4096,384]{2,1,0:T(8,128)(2,1)S(1)} %copy-done), kind=kOutput, calls=%fused_computation.8 | convolution fusion | flops 6442450944 | bytes 23068672 | tf_op jit(solution)/shard_map/dot_general | solution.py:40
  293.4 10.0 %fusion.6 = bf16[2048,384]{1,0:T(8,128)(2,1)} fusion(bf16[2048,4096]{1,0:T(8,128)(2,1)S(1)} %bitcast.40, bf16[1,4096,384]{2,1,0:T(8,128)(2,1)S(1)} %copy-done.4, f32[2048,384]{1,0:T(8,128)S(1)} %fusion.3), kind=kOutput, calls=%fused_computation.13 | convolution fusion | flops 6447169536 | bytes 24641536 | tf_op jit(solution)/shard_map/dot_general | solution.py:41
  303.5 0.1 copy.38
  303.6 0.1 reshape.69
  303.7 1.5 fusion
  305.2 0.1 all_to_all.12
  305.3 12.0 %all_to_all.16 = bf16[32,1,64]{2,1,0:T(2,128)(2,1)S(1)} all-to-all(bf16[32,1,64]{2,1,0:T(2,128)(2,1)S(1)} %all_to_all.12), channel_id=1, replica_groups=mesh['head'=4,'expert'=32] {'expert'}, dimensions={0} | all-to-all | bytes 8192 | tf_op jit(solution)/shard_map/all_to_all | solution.py:34
  317.3 0.7 convert_reduce_fusion.1
  318.1 46.6 %all-gather.2.cloned.1.call-done = bf16[2048,1536]{1,0:T(8,128)(2,1)} async-done(((bf16[2048,384]{1,0:T(8,128)(2,1)}), bf16[2048,1536]{1,0:T(8,128)(2,1)}) %all-gather.2.cloned.1.call-update) | async-done | bytes 6291472 | tf_op jit(solution)/shard_map/all_gather | solution.py:47
  364.7 8.3 %fusion.5 = f32[1,384,1536]{2,1,0:T(8,128)} fusion(bf16[2048,1536]{1,0:T(8,128)(2,1)} %all-gather.2.cloned.1.call-done, bf16[2048,384]{1,0:T(8,128)(2,1)} %fusion.6, f32[2048]{0:T(1024)S(1)} %reshape.68, f32[]{:T(128)} %get-tuple-element.5), kind=kOutput, calls=%fused_computation.12 | convolution fusion | flops 2418868224 | bytes 10231812 | tf_op jit(solution)/shard_map/dot_general | solution.py:45
  (25 shorter events, 0.4 us)
Async XLA Ops:
  6.5 278.0 %copy-start = (bf16[1,4096,384]{2,1,0:T(8,128)(2,1)S(1)}, bf16[1,4096,384]{2,1,0:T(8,128)(2,1)}, u32[]{:S(2)}) copy-start(bf16[1,4096,384]{2,1,0:T(8,128)(2,1)} %param.12) | copy-start | bytes 9437188
  6.5 6.3 %copy-start.2 = (s32[128,8]{0,1:T(8,128)S(1)}, s32[128,8]{0,1:T(8,128)}, u32[]{:S(2)}) copy-start(s32[128,8]{0,1:T(8,128)} %param.10) | copy-start | bytes 12292
  6.5 67.3 %all-reduce.2.cloned.1.call-start = ((), (), s32[]{:S(2)}) async-start(), calls=%async_computation.2 | async-start | bytes 4194304 | tf_op jit(solution)/shard_map/psum | solution.py:10
  12.8 351.9 %all-gather.2.cloned.1.call-start = ((), (), s32[]{:S(2)}) async-start(), calls=%async_computation.3 | async-start | bytes 7864320 | tf_op jit(solution)/shard_map/all_gather | solution.py:47
  284.5 8.9 %copy-start.4 = (bf16[1,4096,384]{2,1,0:T(8,128)(2,1)S(1)}, bf16[1,4096,384]{2,1,0:T(8,128)(2,1)}, u32[]{:S(2)}) copy-start(bf16[1,4096,384]{2,1,0:T(8,128)(2,1)} %param.13) | copy-start | bytes 9437188
  293.4 10.1 %copy-start.3 = (bf16[128,8]{0,1:T(8,128)(2,1)S(1)}, bf16[128,8]{0,1:T(8,128)(2,1)}, u32[]{:S(2)}) copy-start(bf16[128,8]{0,1:T(8,128)(2,1)} %param.11) | copy-start | bytes 6148
  364.7 8.3 %copy-start.1 = (bf16[1,4096,384]{2,1,0:T(8,128)(2,1)S(1)}, bf16[1,4096,384]{2,1,0:T(8,128)(2,1)}, u32[]{:S(2)}) copy-start(bf16[1,4096,384]{2,1,0:T(8,128)(2,1)} %param.12) | copy-start | bytes 9437188
Sparse Core Ops, SparseCore 0:
  12.9 60.8 all-reduce.1
  303.6 61.0 all-gather.1
where the time goes:
time: 380 us
  blocking collectives  208 us (55%)
  waiting for transfers between devices  86.1 us (23%)
  matrix products  47.2 us (12%)
  other arithmetic  23.7 us (6%)
  between operations  13.5 us (4%)
    all_to_all x1, blocking collectives, body(): lax.all_to_all(outgoing, 'expert', split_axis=0, concat_axis=0, tiled=True)  196 us
    all_gather x1, waiting for transfers between devices, body(): lax.all_gather(keys, 'head', axis=1, tiled=True)  46.6 us
    psum x1, waiting for transfers between devices, body(): mixed = residual.astype(jnp.float32) + lax.psum(partial_value, 'head')  39.5 us
    dot_general x1, matrix products, body(): jnp.dot(pick_rows, normed, preferred_element_type=jnp.float32)  12.3 us
    all_to_all x1, blocking collectives, body(): lax.all_to_all(out_weight, 'expert', split_axis=0, concat_axis=0, tiled=T...  12 us
    reduce_sum x1, other arithmetic, body(): jnp.sum(select.reshape(owners * capacity, tok_rows, picks).astype(jnp.flo...  11.5 us
    dot_general x1, matrix products, body(): up = jnp.dot(received, w_up, preferred_element_type=jnp.float32)  10 us
    another operation x3, other arithmetic  9.15 us
  transfers between devices with their start and end apart: 2, of which 2 were waited for; matrix products, arithmetic and copies ran while one was open for 6% of the time, Pallas kernels for 0%

commit v1 on v0

--- a/solution.py
+++ b/solution.py
@@ -2,6 +2,13 @@
 import jax.numpy as jnp
 from jax import lax
 from jax.sharding import PartitionSpec as P
+
+
+def gather_over(value, axis, dim):
+    count = lax.axis_size(axis)
+    blocks = jnp.stack([value for _ in range(count)])
+    blocks = lax.all_to_all(blocks, axis, split_axis=0, concat_axis=0)
+    return jnp.concatenate(blocks, axis=dim)
 
 
 def body(attn, o_weight, residual, expert_ids, route_weight, gate_weight, up_weight):
@@ -44,7 +51,7 @@
     total = jnp.sum(weights)
     block = lax.dot_general(
         scaled,
-        lax.all_gather(keys, "head", axis=1, tiled=True),
+        gather_over(keys, "head", 1),
         (((0,), (0,)), ((), ())),
         preferred_element_type=jnp.float32,
     )

time: 380 us -> 514 us (1.35)
  waiting for transfers between devices: 86.1 us -> 353 us
  blocking collectives: 208 us -> 0 us
  starting transfers between devices: 0.04 us -> 64.8 us
  matrix products: 47.2 us -> 53.2 us
    all_to_all x0 -> x3, waiting for transfers between devices: none -> 313 us  [the longest x1 244 us: body(): lax.all_to_all(outgoing, 'expert', split_axis=0, concat_axis=0, tiled=True)]
    all_to_all x2 -> x0, blocking collectives: 208 us -> none  [the longest x1 196 us: body(): lax.all_to_all(outgoing, 'expert', split_axis=0, concat_axis=0, tiled=True)]
    all_to_all x0 -> x3, starting transfers between devices: none -> 64.8 us  [the longest x1 48.2 us: body(): lax.all_to_all(out_weight, 'expert', split_axis=0, concat_axis=0, tiled=T...]
    all_gather x1 -> x0, waiting for transfers between devices: 46.6 us -> none  [body(): lax.all_gather(keys, 'head', axis=1, tiled=True)]
  transfers between devices with their start and end apart: 2 -> 4, of which waited for: 2 -> 3; matrix products, arithmetic and copies ran while one was open for 6% -> 10% of each run, Pallas kernels for 0% -> 0%
where the time goes in v1:
time: 514 us
  waiting for transfers between devices  353 us (69%)
  starting transfers between devices  64.8 us (13%)
  matrix products  53.2 us (10%)
  other arithmetic  23.6 us (5%)
  between operations  13.6 us (3%)
  local copies, waits for them, and re-layouts  5.95 us (1%)
    all_to_all x1, waiting for transfers between devices, body(): lax.all_to_all(outgoing, 'expert', split_axis=0, concat_axis=0, tiled=True)  244 us
    all_to_all x1, waiting for transfers between devices, gather_over(): blocks = lax.all_to_all(blocks, axis, split_axis=0, concat_axis=0)  69.1 us
    all_to_all x1, starting transfers between devices, body(): lax.all_to_all(out_weight, 'expert', split_axis=0, concat_axis=0, tiled=T...  48.2 us
    psum x1, waiting for transfers between devices, body(): mixed = residual.astype(jnp.float32) + lax.psum(partial_value, 'head')  39.6 us
    dot_general x1, matrix products, body(): up = jnp.dot(received, w_up, preferred_element_type=jnp.float32)  12.6 us
    dot_general x1, matrix products, body(): jnp.dot(pick_rows, normed, preferred_element_type=jnp.float32)  12.3 us
    dot_general x1, matrix products, body(): gate = jnp.dot(received, w_gate, preferred_element_type=jnp.float32)  12.1 us
    reduce_sum x1, other arithmetic, body(): jnp.sum(select.reshape(owners * capacity, tok_rows, picks).astype(jnp.flo...  11.5 us
  transfers between devices with their start and end apart: 4, of which 3 were waited for; matrix products, arithmetic and copies ran while one was open for 10% of the time, Pallas kernels for 0%

profile of v1, /device:TPU:1, one launch (start us, length us, event | category | flops | bytes accessed | tf_op | source)
XLA Modules:
  0.0 513.9 jit_solution(13564832426878853049)
XLA Ops:
  6.5 6.2 %fusion.16 = f32[128,4096]{1,0:T(8,128)} fusion(bf16[128,1024]{1,0:T(8,128)(2,1)} %param.7, bf16[1024,4096]{1,0:T(8,128)(2,1)} %param.8), kind=kOutput, calls=%fused_computation.33 | convolution fusion | flops 1073741824 | bytes 10747904 | tf_op jit(solution)/shard_map/dot_general | solution.py:15
  12.8 0.1 copy.36
  13.1 9.0 %reduce-window.6 = s32[32,8,128]{2,1,0:T(8,128)S(1)} reduce-window(s32[32,8,128]{2,1,0:T(8,128)S(1)} %fusion.15, s32[]{:T(128)} %constant.7.clone.1), window={size=1x1x128 pad=0_0x0_0x127_0}, to_apply=%region_0.0 | reduce-window | flops 4161536 | bytes 262148 | tf_op jit(solution)/shard_map/reduce-window
  22.2 0.1 copy.38
  22.4 0.1 broadcast_add_fusion
  22.7 11.5 %convert_reduce_fusion = bf16[2048,128]{1,0:T(8,128)(2,1)} fusion(s32[128,8]{0,1:T(8,128)S(1)} %multiply_add_fusion.1), kind=kLoop, calls=%fused_computation.2 | loop fusion | flops 6029312 | bytes 528384 | tf_op jit(solution)/shard_map/reduce_sum | solution.py:30
  34.3 39.6 %all-reduce.2.cloned.1.call-done = f32[128,4096]{1,0:T(8,128)} async-done(((f32[128,4096]{1,0:T(8,128)}), f32[128,4096]{1,0:T(8,128)}) %all-reduce.2.cloned.1.call-update) | async-done | bytes 2097168 | tf_op jit(solution)/shard_map/psum | solution.py:17
  73.9 2.2 multiply_reduce_fusion
  76.1 12.3 %convolution_convert_fusion = bf16[2048,4096]{1,0:T(8,128)(2,1)} fusion(f32[128,4096]{1,0:T(8,128)} %all-reduce.2.cloned.1.call-done, bf16[128,4096]{1,0:T(8,128)(2,1)} %param.9, f32[128]{0:T(128)S(1)} %add_rsqrt_fusion, bf16[2048,128]{1,0:T(8,128)(2,1)} %convert_reduce_fusion), kind=kOutput, calls=%fused_computation | convolution fusion | flops 2157969408 | bytes 20447744 | tf_op jit(solution)/shard_map/dot_general | solution.py:33
  88.4 9.5 %all-to-all-start = ((bf16[32,64,4096]{2,1,0:T(8,128)(2,1)}), bf16[32,64,4096]{2,1,0:T(8,128)(2,1)}, u32[]{:S(2)}, u32[]{:S(2)}) async-start(bf16[32,64,4096]{2,1,0:T(8,128)(2,1)} %bitcast.41), calls=%async_computation | async-start | bytes 33554432 | tf_op jit(solution)/shard_map/all_to_all | solution.py:40
  98.0 0.1 copy.41
  98.1 0.1 reshape.79
  98.2 1.5 fusion
  99.7 0.7 all_to_all.16
  100.4 244.0 %all-to-all-done = bf16[32,64,4096]{2,1,0:T(8,128)(2,1)} async-done(((bf16[32,64,4096]{2,1,0:T(8,128)(2,1)}), bf16[32,64,4096]{2,1,0:T(8,128)(2,1)}, u32[]{:S(2)}, u32[]{:S(2)}) %all-to-all-start) | async-done | bytes 16777248 | tf_op jit(solution)/shard_map/all_to_all | solution.py:40
  344.4 48.2 %all-to-all-start.1 = ((bf16[32,1,64]{2,1,0:T(2,128)(2,1)}), bf16[32,1,64]{2,1,0:T(2,128)(2,1)S(1)}, u32[]{:S(2)}, u32[]{:S(2)}) async-start(bf16[32,1,64]{2,1,0:T(2,128)(2,1)} %all_to_all.16), calls=%async_computation.1 | async-start | bytes 32768 | tf_op jit(solution)/shard_map/all_to_all | solution.py:41
  392.5 12.1 %fusion.3 = f32[2048,384]{1,0:T(8,128)S(1)} fusion(bf16[2048,4096]{1,0:T(8,128)(2,1)} %bitcast.3, bf16[1,4096,384]{2,1,0:T(8,128)(2,1)S(1)} %copy-done), kind=kOutput, calls=%fused_computation.8 | convolution fusion | flops 6442450944 | bytes 23068672 | tf_op jit(solution)/shard_map/dot_general | solution.py:47
  404.6 12.6 %fusion.6 = bf16[2048,384]{1,0:T(8,128)(2,1)S(1)} fusion(bf16[2048,4096]{1,0:T(8,128)(2,1)} %bitcast.3, bf16[1,4096,384]{2,1,0:T(8,128)(2,1)S(1)} %copy-done.5, f32[2048,384]{1,0:T(8,128)S(1)} %fusion.3), kind=kOutput, calls=%fused_computation.13 | convolution fusion | flops 6447169536 | bytes 24641536 | tf_op jit(solution)/shard_map/dot_general | solution.py:48
  417.2 0.8 copy.43
  418.0 3.5 stack.2
  421.4 7.1 %all-to-all-start.2 = ((bf16[4,2048,384]{1,2,0:T(8,128)(2,1)}), bf16[4,2048,384]{1,2,0:T(8,128)(2,1)}, u32[]{:S(2)}, u32[]{:S(2)}) async-start(bf16[4,2048,384]{1,2,0:T(8,128)(2,1)} %stack.2), calls=%async_computation.2 | async-start | bytes 12582912 | tf_op jit(solution)/shard_map/all_to_all | solution.py:10
  428.5 0.7 convert_reduce_fusion.1
  429.3 69.1 %all-to-all-done.2 = bf16[4,2048,384]{1,2,0:T(8,128)(2,1)} async-done(((bf16[4,2048,384]{1,2,0:T(8,128)(2,1)}), bf16[4,2048,384]{1,2,0:T(8,128)(2,1)}, u32[]{:S(2)}, u32[]{:S(2)}) %all-to-all-start.2) | async-done | bytes 6291488 | tf_op jit(solution)/shard_map/all_to_all | solution.py:10
  498.4 8.6 %fusion.5 = f32[1,384,1536]{2,1,0:T(8,128)} fusion(bf16[2048,1536]{0,1:T(8,128)(2,1)} %bitcast.8, bf16[2048,384]{1,0:T(8,128)(2,1)} %copy-done.2, f32[2048]{0:T(1024)S(1)} %reshape.78, f32[]{:T(128)} %get-tuple-element.5), kind=kOutput, calls=%fused_computation.12 | convolution fusion | flops 2418868224 | bytes 10231812 | tf_op jit(solution)/shard_map/dot_general | solution.py:52
  (30 shorter events, 0.7 us)
Async XLA Ops:
  6.5 386.0 %copy-start = (bf16[1,4096,384]{2,1,0:T(8,128)(2,1)S(1)}, bf16[1,4096,384]{2,1,0:T(8,128)(2,1)}, u32[]{:S(2)}) copy-start(bf16[1,4096,384]{2,1,0:T(8,128)(2,1)} %param.12) | copy-start | bytes 9437188
  6.5 6.2 %copy-start.3 = (s32[128,8]{0,1:T(8,128)S(1)}, s32[128,8]{0,1:T(8,128)}, u32[]{:S(2)}) copy-start(s32[128,8]{0,1:T(8,128)} %param.10) | copy-start | bytes 12292
  6.5 67.3 %all-reduce.2.cloned.1.call-start = ((), (), s32[]{:S(2)}) async-start(), calls=%async_computation.3 | async-start | bytes 4194304 | tf_op jit(solution)/shard_map/psum | solution.py:17
  88.4 9.6 %copy-start.4 = (bf16[128,8]{0,1:T(8,128)(2,1)S(1)}, bf16[128,8]{0,1:T(8,128)(2,1)}, u32[]{:S(2)}) copy-start(bf16[128,8]{0,1:T(8,128)(2,1)} %param.11) | copy-start | bytes 6148
  88.4 255.9 %all-to-all-start = ((bf16[32,64,4096]{2,1,0:T(8,128)(2,1)}), bf16[32,64,4096]{2,1,0:T(8,128)(2,1)}, u32[]{:S(2)}, u32[]{:S(2)}) async-start(bf16[32,64,4096]{2,1,0:T(8,128)(2,1)} %bitcast.41), calls=%async_computation | async-start | bytes 33554432 | tf_op jit(solution)/shard_map/all_to_all | solution.py:40
  344.4 73.6 %all-to-all-start.1 = ((bf16[32,1,64]{2,1,0:T(2,128)(2,1)}), bf16[32,1,64]{2,1,0:T(2,128)(2,1)S(1)}, u32[]{:S(2)}, u32[]{:S(2)}) async-start(bf16[32,1,64]{2,1,0:T(2,128)(2,1)} %all_to_all.16), calls=%async_computation.1 | async-start | bytes 32768 | tf_op jit(solution)/shard_map/all_to_all | solution.py:41
  392.5 12.1 %copy-start.5 = (bf16[1,4096,384]{2,1,0:T(8,128)(2,1)S(1)}, bf16[1,4096,384]{2,1,0:T(8,128)(2,1)}, u32[]{:S(2)}) copy-start(bf16[1,4096,384]{2,1,0:T(8,128)(2,1)} %param.13) | copy-start | bytes 9437188
  417.2 4.3 copy-start.2
  421.4 77.0 %all-to-all-start.2 = ((bf16[4,2048,384]{1,2,0:T(8,128)(2,1)}), bf16[4,2048,384]{1,2,0:T(8,128)(2,1)}, u32[]{:S(2)}, u32[]{:S(2)}) async-start(bf16[4,2048,384]{1,2,0:T(8,128)(2,1)} %stack.2), calls=%async_computation.2 | async-start | bytes 12582912 | tf_op jit(solution)/shard_map/all_to_all | solution.py:10
  498.4 8.6 %copy-start.1 = (bf16[1,4096,384]{2,1,0:T(8,128)(2,1)S(1)}, bf16[1,4096,384]{2,1,0:T(8,128)(2,1)}, u32[]{:S(2)}) copy-start(bf16[1,4096,384]{2,1,0:T(8,128)(2,1)} %param.12) | copy-start | bytes 9437188
Sparse Core Ops, SparseCore 0:
  12.9 60.9 all-reduce.1
